TPU v7x, 32 devices: a whole 2x2x4 slice. The times are simulated.
32 devices in a mesh: row: 2 (over y), col: 16 (over z, x, core).
Axes of the slice: x: 2, y: 2, z: 4, core: 2. Of those that a mesh axis runs over, the one named last changes fastest.
Arguments:
- coefficients: float32 [2, 2, 8, 2048, 512], P(None, None, None, ('row', 'col')), may hold values from -6 to 6
- vertical_modes: float32 [512, 512], replicated, may hold values from -0.25 to 0.25
- mode_slopes: float32 [512, 512], replicated, may hold values from -0.25 to 0.25
- dual_modes: float32 [512, 512], replicated, may hold values from -0.25 to 0.25
- eigenvalues: float32 [512], replicated, may hold values from 0.01 to 10
- velocity: float32 [3, 512, 2048], P(None, 'col'), may hold values from -5 to 5
- gradient: float32 [2, 512], P(None, 'col'), may hold values from 0.2 to 2
- span_wavenumbers: float32 [8], replicated, may hold values from 0 to 2
- implicit_rates: float32 [2], replicated, may hold values from 0.02 to 0.2
- time_step: float32 [], replicated, may hold values from 0.2 to 0.5
Outputs:
- new_coefficients: float32 [2, 2, 8, 2048, 512], P(None, None, None, ('row', 'col'))
All inputs are finite; a program needn't handle non-finite values.
Results may differ from a plain program's by a relative error of at most 0.00005.
Values sent between devices are 32-bit elements; how exact they have to be, the bound alone decides.
A program may use at most 128 MiB of HBM per device.

v0:
```python
import math
import jax
import jax.numpy as jnp
from jax import lax
from jax.sharding import PartitionSpec as P

highest = lax.Precision.HIGHEST
lane_width = 128


def signed_waves(length):
    indices = jnp.arange(length, dtype=jnp.int32)
    return jnp.where(indices < length // 2, indices, indices - length)


def phase_table(row_total, col_total, period, direction):
    left_index = jnp.arange(row_total, dtype=jnp.int32)[:, None]
    right_index = jnp.arange(col_total, dtype=jnp.int32)[None, :]
    angles = (left_index * right_index % period).astype(jnp.float32) * (2.0 * math.pi / period)
    return (jnp.cos(angles), direction * jnp.sin(angles))


def contract(form, left_real, left_imag, right_real, right_imag):
    product_real = jnp.einsum(form, left_real, right_real, precision=highest) - jnp.einsum(
        form, left_imag, right_imag, precision=highest
    )
    product_imag = jnp.einsum(form, left_real, right_imag, precision=highest) + jnp.einsum(
        form, left_imag, right_real, precision=highest
    )
    return (product_real, product_imag)


def twisted(real_in, imag_in, twist_real, twist_imag):
    return (
        real_in * twist_real - imag_in * twist_imag,
        real_in * twist_imag + imag_in * twist_real,
    )


def inverse_transform(real_in, imag_in, length):
    short_size = length // lane_width
    scale = 1.0 / math.sqrt(length)
    short_real, short_imag = phase_table(short_size, short_size, short_size, 1.0)
    twist_real, twist_imag = phase_table(short_size, lane_width, length, 1.0)
    wide_real, wide_imag = phase_table(lane_width, lane_width, lane_width, 1.0)
    middle_real, middle_imag = contract("...ef,ed->...df", real_in, imag_in, short_real, short_imag)
    middle_real, middle_imag = twisted(middle_real, middle_imag, twist_real, twist_imag)
    return contract(
        "...df,fc->...dc", middle_real, middle_imag, wide_real * scale, wide_imag * scale
    )


def forward_transform(real_in, imag_in, length):
    short_size = length // lane_width
    scale = 1.0 / math.sqrt(length)
    short_real, short_imag = phase_table(short_size, short_size, short_size, -1.0)
    twist_real, twist_imag = phase_table(short_size, lane_width, length, -1.0)
    wide_real, wide_imag = phase_table(lane_width, lane_width, lane_width, -1.0)
    middle_real, middle_imag = contract("...dc,cf->...df", real_in, imag_in, wide_real, wide_imag)
    middle_real, middle_imag = twisted(middle_real, middle_imag, twist_real, twist_imag)
    return contract(
        "...df,de->...ef", middle_real, middle_imag, short_real * scale, short_imag * scale
    )


def on_device(
    coefficients,
    vertical_modes,
    mode_slopes,
    dual_modes,
    eigenvalues,
    velocity,
    gradient,
    span_wavenumbers,
    implicit_rates,
    time_step,
):
    row_count = lax.axis_size("row")
    col_count = lax.axis_size("col")
    local_waves = coefficients.shape[3]
    total_points = local_waves * row_count * col_count
    short_size = total_points // lane_width
    first_wave = (lax.axis_index("row") * col_count + lax.axis_index("col")) * local_waves
    signed = signed_waves(total_points)
    zonal_waves = signed.astype(jnp.float32) * (2.0 * math.pi / total_points)
    own_waves = lax.dynamic_slice_in_dim(zonal_waves, first_wave, local_waves)
    value_real = jnp.einsum("sqpj,zj->zsqp", coefficients[:, 0], vertical_modes, precision=highest)
    value_imag = jnp.einsum("sqpj,zj->zsqp", coefficients[:, 1], vertical_modes, precision=highest)
    slope_real = jnp.einsum("sqpj,zj->zsqp", coefficients[:, 0], mode_slopes, precision=highest)
    slope_imag = jnp.einsum("sqpj,zj->zsqp", coefficients[:, 1], mode_slopes, precision=highest)
    fields = (
        lax.all_to_all(value_real, "col", split_axis=0, concat_axis=3, tiled=True),
        lax.all_to_all(value_imag, "col", split_axis=0, concat_axis=3, tiled=True),
        lax.all_to_all(slope_real, "col", split_axis=0, concat_axis=3, tiled=True),
        lax.all_to_all(slope_imag, "col", split_axis=0, concat_axis=3, tiled=True),
    )
    fields = (
        lax.all_to_all(fields[0], "row", split_axis=2, concat_axis=3, tiled=True),
        lax.all_to_all(fields[1], "row", split_axis=2, concat_axis=3, tiled=True),
        lax.all_to_all(fields[2], "row", split_axis=2, concat_axis=3, tiled=True),
        lax.all_to_all(fields[3], "row", split_axis=2, concat_axis=3, tiled=True),
    )
    level_rows = fields[0].shape[0]
    span_rows = fields[0].shape[2]
    grid_shape = (level_rows, 2, span_rows, short_size, lane_width)
    value_real = fields[0].reshape(grid_shape)
    value_imag = fields[1].reshape(grid_shape)
    slope_real = fields[2].reshape(grid_shape)
    slope_imag = fields[3].reshape(grid_shape)
    wave_grid = zonal_waves.reshape(short_size, lane_width)
    scalar_real, scalar_imag = inverse_transform(value_real, value_imag, total_points)
    zonal_real, zonal_imag = inverse_transform(
        -wave_grid * value_imag, wave_grid * value_real, total_points
    )
    rise_real, rise_imag = inverse_transform(slope_real, slope_imag, total_points)
    flow = jnp.swapaxes(velocity.reshape(3, level_rows, lane_width, short_size), -1, -2)
    zonal_flow = flow[0][:, None, None]
    span_flow = flow[1][:, None, None]
    rise_flow = flow[2][:, None, None]
    span_waves = lax.dynamic_slice_in_dim(
        span_wavenumbers, lax.axis_index("row") * span_rows, span_rows
    )[None, None, :, None, None]
    background = jnp.transpose(gradient)[:, :, None, None, None]
    advect_real = (
        zonal_flow * zonal_real
        - span_waves * span_flow * scalar_imag
        + rise_flow * rise_real
        + rise_flow * background
    )
    advect_imag = (
        zonal_flow * zonal_imag + span_waves * span_flow * scalar_real + rise_flow * rise_imag
    )
    spectra_real, spectra_imag = forward_transform(advect_real, advect_imag, total_points)
    retained = (
        (jnp.abs(signed) <= total_points // 3).astype(jnp.float32).reshape(short_size, lane_width)
    )
    flat_shape = (level_rows, 2, span_rows, total_points)
    spectra_real = (spectra_real * retained).reshape(flat_shape)
    spectra_imag = (spectra_imag * retained).reshape(flat_shape)
    returned_real, returned_imag = (
        lax.all_to_all(
            lax.all_to_all(spectra_real, "row", split_axis=3, concat_axis=2, tiled=True),
            "col",
            split_axis=3,
            concat_axis=0,
            tiled=True,
        ),
        lax.all_to_all(
            lax.all_to_all(spectra_imag, "row", split_axis=3, concat_axis=2, tiled=True),
            "col",
            split_axis=3,
            concat_axis=0,
            tiled=True,
        ),
    )
    forcing_real = jnp.einsum("zsqp,jz->sqpj", returned_real, dual_modes, precision=highest)
    forcing_imag = jnp.einsum("zsqp,jz->sqpj", returned_imag, dual_modes, precision=highest)
    forcing = jnp.stack([forcing_real, forcing_imag], 1)
    denominator = 1.0 + implicit_rates[:, None, None, None, None] * (
        eigenvalues[None, None, None, None, :]
        + own_waves[None, None, None, :, None] ** 2
        + span_wavenumbers[None, None, :, None, None] ** 2
    )
    return (coefficients - time_step * forcing) / denominator


def solution(mesh):
    in_specs = (
        P(None, None, None, ("row", "col"), None),
        P(),
        P(),
        P(),
        P(),
        P(None, "col", None),
        P(None, "col"),
        P(),
        P(),
        P(),
    )
    out_specs = P(None, None, None, ("row", "col"), None)
    return jax.shard_map(
        on_device, mesh=mesh, in_specs=in_specs, out_specs=out_specs, check_vma=False
    )
```

profile of v0, /device:TPU:15, one launch (start us, length us, event | category | flops | bytes accessed | tf_op | source)
XLA Modules:
  0.0 696.5 jit_solution(4996307598044424374)
XLA Ops:
  10.1 5.5 reshape.198
  15.6 6.6 all-to-all-start.2
  31.0 5.5 reshape.200
  36.5 33.1 %all-to-all-done.2 = f32[16,1,32768]{2,1,0:T(1,128)} async-done(((f32[16,1,32768]{2,1,0:T(1,128)}), f32[16,1,32768]{2,1,0:T(1,128)}, u32[]{:S(2)}, u32[]{:S(2)}) %all-to-all-start.2) | async-done | bytes 2097184 | tf_op jit(solution)/shard_map/all_to_all | solution.py:92
  69.7 5.5 all-to-all-start
  84.1 5.5 reshape.194
  89.6 33.0 %all-to-all-done = f32[16,1,32768]{2,1,0:T(1,128)} async-done(((f32[16,1,32768]{2,1,0:T(1,128)}), f32[16,1,32768]{2,1,0:T(1,128)}, u32[]{:S(2)}, u32[]{:S(2)}) %all-to-all-start) | async-done | bytes 2097184 | tf_op jit(solution)/shard_map/all_to_all | solution.py:93
  136.3 5.5 reshape.196
  141.8 33.2 %all-to-all-done.4 = f32[16,1,32768]{2,1,0:T(1,128)} async-done(((f32[16,1,32768]{2,1,0:T(1,128)}), f32[16,1,32768]{2,1,0:T(1,128)}, u32[]{:S(2)}, u32[]{:S(2)}) %all-to-all-start.4) | async-done | bytes 2097184 | tf_op jit(solution)/shard_map/all_to_all | solution.py:94
  175.0 5.2 all-to-all-start.6
  183.1 7.3 %reduce.2 = f32[16,32768]{1,0:T(8,128)S(1)} reduce(f32[16,1,32768]{2,1,0:T(1,128)} %all-to-all-done.2, f32[]{:T(128)} %broadcast.567), dimensions={1}, to_apply=%all_to_all.155.reduce_sub_computation | reduce | bytes 4194308 | tf_op jit(solution)/shard_map/all_to_all | solution.py:92
  193.4 6.6 copy.141
  205.2 22.4 %all-to-all-done.6 = f32[16,1,32768]{2,1,0:T(1,128)} async-done(((f32[16,1,32768]{2,1,0:T(1,128)}), f32[16,1,32768]{2,1,0:T(1,128)}, u32[]{:S(2)}, u32[]{:S(2)}) %all-to-all-start.6) | async-done | bytes 2097184 | tf_op jit(solution)/shard_map/all_to_all | solution.py:95
  227.6 5.4 all-to-all-start.3
  239.4 7.3 %reduce.3 = f32[16,32768]{1,0:T(8,128)S(1)} reduce(f32[16,1,32768]{2,1,0:T(1,128)} %all-to-all-done, f32[]{:T(128)} %broadcast.567), dimensions={1}, to_apply=%all_to_all.148.reduce_sub_computation | reduce | bytes 4194308 | tf_op jit(solution)/shard_map/all_to_all | solution.py:93
  249.7 6.6 copy.140
  256.3 5.2 reshape.190
  266.6 7.3 %reduce = f32[16,32768]{1,0:T(8,128)S(1)} reduce(f32[16,1,32768]{2,1,0:T(1,128)} %all-to-all-done.4, f32[]{:T(128)} %broadcast.567), dimensions={1}, to_apply=%all_to_all.162.reduce_sub_computation | reduce | bytes 4194308 | tf_op jit(solution)/shard_map/all_to_all | solution.py:94
  276.9 6.6 copy.142
  288.7 7.3 %reduce.1 = f32[16,32768]{1,0:T(8,128)S(1)} reduce(f32[16,1,32768]{2,1,0:T(1,128)} %all-to-all-done.6, f32[]{:T(128)} %broadcast.567), dimensions={1}, to_apply=%all_to_all.169.reduce_sub_computation | reduce | bytes 4194308 | tf_op jit(solution)/shard_map/all_to_all | solution.py:95
  299.3 6.6 copy.143
  351.1 6.7 all-to-all-done.5
  357.9 5.9 all-to-all-start.7
  446.2 6.4 copy.144
  452.6 8.8 %reshape.206 = f32[2,1,262144]{2,1,0:T(1,128)} reshape(f32[2048,2,4,32]{3,2,1,0:T(4,128)} %bitcast.251) | data formatting | bytes 4194304
  473.5 6.4 copy.148
  479.9 8.8 %reshape.202 = f32[2,1,262144]{2,1,0:T(1,128)} reshape(f32[2048,2,4,32]{3,2,1,0:T(4,128)} %bitcast.252) | data formatting | bytes 4194304
  488.7 6.2 all-to-all-start.10
  495.0 8.1 %reduce.6 = f32[2,262144]{1,0:T(2,128)S(1)} reduce(f32[2,1,262144]{2,1,0:T(1,128)} %all-to-all-done.8, f32[]{:T(128)} %broadcast.567), dimensions={1}, to_apply=%all_to_all.176.reduce_sub_computation | reduce | bytes 4194308 | tf_op jit(solution)/shard_map/all_to_all | solution.py:142
  503.1 8.2 %reshape.207 = f32[2048,2,4,32]{3,2,1,0:T(4,128)} reshape(f32[2,262144]{1,0:T(2,128)S(1)} %reduce.6) | data formatting | bytes 4194304
  511.4 6.9 copy.145
  520.2 7.5 %copy.116 = f32[32,2,8,1024]{0,2,1,3:T(8,128)} copy(f32[32,2,8,1024]{3,0,2,1:T(8,128)} %bitcast.267) | data formatting | bytes 4194304 | tf_op jit(solution)/shard_map/all_to_all | solution.py:142
  527.7 8.6 %reshape.208 = f32[16,1,32768]{2,1,0:T(1,128)} reshape(f32[1024,2,8,32]{3,2,1,0:T(8,128)} %bitcast.254) | data formatting | bytes 4194304
  536.3 7.7 %all-to-all-start.9 = ((f32[16,1,32768]{2,1,0:T(1,128)}), f32[16,1,32768]{2,1,0:T(1,128)}, u32[]{:S(2)}, u32[]{:S(2)}) async-start(f32[16,1,32768]{2,1,0:T(1,128)} %reshape.208), calls=%async_computation.9 | async-start | bytes 4194304 | tf_op jit(solution)/shard_map/all_to_all | solution.py:141
  544.0 8.1 %reduce.4 = f32[2,262144]{1,0:T(2,128)S(1)} reduce(f32[2,1,262144]{2,1,0:T(1,128)} %all-to-all-done.10, f32[]{:T(128)} %broadcast.567), dimensions={1}, to_apply=%all_to_all.184.reduce_sub_computation | reduce | bytes 4194308 | tf_op jit(solution)/shard_map/all_to_all | solution.py:149
  552.2 8.2 %reshape.203 = f32[2048,2,4,32]{3,2,1,0:T(4,128)} reshape(f32[2,262144]{1,0:T(2,128)S(1)} %reduce.4) | data formatting | bytes 4194304
  560.4 6.9 copy.149
  569.2 7.5 %copy.123 = f32[32,2,8,1024]{0,2,1,3:T(8,128)} copy(f32[32,2,8,1024]{3,0,2,1:T(8,128)} %bitcast.269) | data formatting | bytes 4194304 | tf_op jit(solution)/shard_map/all_to_all | solution.py:149
  576.7 8.6 %reshape.204 = f32[16,1,32768]{2,1,0:T(1,128)} reshape(f32[1024,2,8,32]{3,2,1,0:T(8,128)} %bitcast.256) | data formatting | bytes 4194304
  585.3 6.1 all-to-all-done.9
  591.4 5.5 all-to-all-start.11
  599.6 7.3 %reduce.7 = f32[16,32768]{1,0:T(8,128)S(1)} reduce(f32[16,1,32768]{2,1,0:T(1,128)} %all-to-all-done.9, f32[]{:T(128)} %broadcast.567), dimensions={1}, to_apply=%all_to_all.180.reduce_sub_computation | reduce | bytes 4194308 | tf_op jit(solution)/shard_map/all_to_all | solution.py:141
  611.7 7.0 copy.156
  618.7 25.6 %all-to-all-done.11 = f32[16,1,32768]{2,1,0:T(1,128)} async-done(((f32[16,1,32768]{2,1,0:T(1,128)}), f32[16,1,32768]{2,1,0:T(1,128)}, u32[]{:S(2)}, u32[]{:S(2)}) %all-to-all-start.11) | async-done | bytes 2097184 | tf_op jit(solution)/shard_map/all_to_all | solution.py:148
  644.3 7.3 %reduce.5 = f32[16,32768]{1,0:T(8,128)S(1)} reduce(f32[16,1,32768]{2,1,0:T(1,128)} %all-to-all-done.11, f32[]{:T(128)} %broadcast.567), dimensions={1}, to_apply=%all_to_all.188.reduce_sub_computation | reduce | bytes 4194308 | tf_op jit(solution)/shard_map/all_to_all | solution.py:148
  656.4 6.9 copy.157
  663.3 15.3 %convolution_bitcast_fusion.1 = f32[2,1,8,64,512]{4,3,2,0,1:T(8,128)S(1)} fusion(f32[512,2,8,64]{3,0,2,1:T(8,128)} %bitcast.259, f32[512,512]{1,0:T(8,128)S(1)} %copy-done.20), kind=kOutput, calls=%fused_computation.57 | convolution fusion | flops 3221225472 | bytes 5242880 | tf_op jit(solution)/shard_map/zsqp,jz->sqpj/dot_general | solution.py:156
  678.7 13.3 %convolution_bitcast_fusion = f32[2,1,8,64,512]{4,3,2,0,1:T(8,128)S(1)} fusion(f32[512,2,8,64]{3,0,2,1:T(8,128)S(1)} %bitcast.260, f32[512,512]{1,0:T(8,128)S(1)} %copy-done.20), kind=kOutput, calls=%fused_computation.56 | convolution fusion | flops 3221225472 | bytes 5242880 | tf_op jit(solution)/shard_map/zsqp,jz->sqpj/dot_general | solution.py:157
  (152 shorter events, 237.5 us)
Async XLA Ops:
  0.0 1.2 copy-start
  15.6 54.1 %all-to-all-start.2 = ((f32[16,1,32768]{2,1,0:T(1,128)}), f32[16,1,32768]{2,1,0:T(1,128)}, u32[]{:S(2)}, u32[]{:S(2)}) async-start(f32[16,1,32768]{2,1,0:T(1,128)} %reshape.198), calls=%async_computation.2 | async-start | bytes 4194304 | tf_op jit(solution)/shard_map/all_to_all | solution.py:92
  36.5 38.7 %copy-start.19 = (f32[512,512]{1,0:T(8,128)S(1)}, f32[512,512]{1,0:T(8,128)}, u32[]{:S(2)}) copy-start(f32[512,512]{1,0:T(8,128)} %param.12) | copy-start | bytes 3145732
  69.7 52.9 %all-to-all-start = ((f32[16,1,32768]{2,1,0:T(1,128)}), f32[16,1,32768]{2,1,0:T(1,128)}, u32[]{:S(2)}, u32[]{:S(2)}) async-start(f32[16,1,32768]{2,1,0:T(1,128)} %reshape.200), calls=%async_computation | async-start | bytes 4194304 | tf_op jit(solution)/shard_map/all_to_all | solution.py:93
  122.5 52.4 %all-to-all-start.4 = ((f32[16,1,32768]{2,1,0:T(1,128)}), f32[16,1,32768]{2,1,0:T(1,128)}, u32[]{:S(2)}, u32[]{:S(2)}) async-start(f32[16,1,32768]{2,1,0:T(1,128)} %reshape.194), calls=%async_computation.4 | async-start | bytes 4194304 | tf_op jit(solution)/shard_map/all_to_all | solution.py:94
  141.8 38.4 %copy-start.24 = (f32[3,32,2048]{2,1,0:T(8,128)S(1)}, f32[3,32,2048]{2,1,0:T(8,128)}, u32[]{:S(2)}) copy-start(f32[3,32,2048]{2,1,0:T(8,128)} %param.15) | copy-start | bytes 2359300
  175.0 52.6 %all-to-all-start.6 = ((f32[16,1,32768]{2,1,0:T(1,128)}), f32[16,1,32768]{2,1,0:T(1,128)}, u32[]{:S(2)}, u32[]{:S(2)}) async-start(f32[16,1,32768]{2,1,0:T(1,128)} %reshape.196), calls=%async_computation.6 | async-start | bytes 4194304 | tf_op jit(solution)/shard_map/all_to_all | solution.py:95
  227.6 34.0 %all-to-all-start.3 = ((f32[32,2,8,1024]{3,1,0,2:T(2,128)}), f32[32,2,8,1024]{3,1,0,2:T(2,128)}, u32[]{:S(2)}, u32[]{:S(2)}) async-start(f32[32,2,8,1024]{3,1,0,2:T(2,128)} %reshape.191), calls=%async_computation.3 | async-start | bytes 4194304 | tf_op jit(solution)/shard_map/all_to_all | solution.py:98
  235.1 2.9 copy-start.26
  235.1 2.9 copy-start.28
  236.3 2.9 copy-start.23
  261.5 67.8 %all-to-all-start.1 = ((f32[32,2,8,1024]{3,1,0,2:T(2,128)}), f32[32,2,8,1024]{3,1,0,2:T(2,128)}, u32[]{:S(2)}, u32[]{:S(2)}) async-start(f32[32,2,8,1024]{3,1,0,2:T(2,128)} %reshape.190), calls=%async_computation.1 | async-start | bytes 4194304 | tf_op jit(solution)/shard_map/all_to_all | solution.py:99
  329.3 28.5 %all-to-all-start.5 = ((f32[32,2,8,1024]{3,1,0,2:T(2,128)}), f32[32,2,8,1024]{3,1,0,2:T(2,128)}, u32[]{:S(2)}, u32[]{:S(2)}) async-start(f32[32,2,8,1024]{3,1,0,2:T(2,128)} %reshape.192), calls=%async_computation.5 | async-start | bytes 4194304 | tf_op jit(solution)/shard_map/all_to_all | solution.py:100
  343.5 1.9 copy-start.7
  343.5 2.2 copy-start.12
  357.9 30.3 %all-to-all-start.7 = ((f32[32,2,8,1024]{3,1,0,2:T(2,128)}), f32[32,2,8,1024]{3,1,0,2:T(2,128)}, u32[]{:S(2)}, u32[]{:S(2)}) async-start(f32[32,2,8,1024]{3,1,0,2:T(2,128)} %reshape.193), calls=%async_computation.7 | async-start | bytes 4194304 | tf_op jit(solution)/shard_map/all_to_all | solution.py:101
  373.1 5.0 copy-start.10
  378.1 3.2 copy-start.3
  397.8 4.4 copy-start.9
  397.8 4.4 copy-start.13
  406.3 2.2 copy-start.8
  406.3 2.2 copy-start.15
  408.6 2.0 copy-start.14
  414.9 2.2 copy-start.4
  423.6 2.4 copy-start.21
  423.6 2.4 copy-start.22
  431.0 2.1 copy-start.17
  431.0 2.2 copy-start.18
  440.7 2.0 copy-start.5
  461.4 27.3 %all-to-all-start.8 = ((f32[2,1,262144]{2,1,0:T(1,128)}), f32[2,1,262144]{2,1,0:T(1,128)}, u32[]{:S(2)}, u32[]{:S(2)}) async-start(f32[2,1,262144]{2,1,0:T(1,128)} %reshape.206), calls=%async_computation.8 | async-start | bytes 4194304 | tf_op jit(solution)/shard_map/all_to_all | solution.py:142
  466.4 3.7 copy-start.6
  488.7 47.5 %all-to-all-start.10 = ((f32[2,1,262144]{2,1,0:T(1,128)}), f32[2,1,262144]{2,1,0:T(1,128)}, u32[]{:S(2)}, u32[]{:S(2)}) async-start(f32[2,1,262144]{2,1,0:T(1,128)} %reshape.202), calls=%async_computation.10 | async-start | bytes 4194304 | tf_op jit(solution)/shard_map/all_to_all | solution.py:149
  536.3 55.1 %all-to-all-start.9 = ((f32[16,1,32768]{2,1,0:T(1,128)}), f32[16,1,32768]{2,1,0:T(1,128)}, u32[]{:S(2)}, u32[]{:S(2)}) async-start(f32[16,1,32768]{2,1,0:T(1,128)} %reshape.208), calls=%async_computation.9 | async-start | bytes 4194304 | tf_op jit(solution)/shard_map/all_to_all | solution.py:141
  585.3 12.3 %copy-start.25 = (f32[512]{0:T(512)S(1)}, f32[512]{0:T(512)}, u32[]{:S(2)}) copy-start(f32[512]{0:T(512)} %param.14) | copy-start | bytes 6148
  585.3 12.6 %copy-start.27 = (f32[2]{0:T(128)S(1)}, f32[2]{0:T(128)}, u32[]{:S(2)}) copy-start(f32[2]{0:T(128)} %param.18) | copy-start | bytes 28
  591.4 52.9 %all-to-all-start.11 = ((f32[16,1,32768]{2,1,0:T(1,128)}), f32[16,1,32768]{2,1,0:T(1,128)}, u32[]{:S(2)}, u32[]{:S(2)}) async-start(f32[16,1,32768]{2,1,0:T(1,128)} %reshape.204), calls=%async_computation.11 | async-start | bytes 4194304 | tf_op jit(solution)/shard_map/all_to_all | solution.py:148
  656.4 6.9 copy-start.20
  663.3 15.4 %copy-start.11 = (f32[16,32,2,8,64]{4,1,0,3,2:T(8,128)S(1)}, f32[16,32,2,8,64]{4,1,0,3,2:T(8,128)}, u32[]{:S(2)}) copy-start(f32[16,32,2,8,64]{4,1,0,3,2:T(8,128)} %copy.157) | copy-start | bytes 6291460
  678.7 13.4 %copy-start.2 = (f32[2,2,8,64,512]{4,3,2,1,0:T(8,128)S(1)}, f32[2,2,8,64,512]{4,3,2,1,0:T(8,128)}, u32[]{:S(2)}) copy-start(f32[2,2,8,64,512]{4,3,2,1,0:T(8,128)} %param.10) | copy-start | bytes 12582916
  678.7 13.4 %copy-start.16 = (f32[2,8,64,512]{3,2,1,0:T(8,128)S(1)}, f32[2,8,64,512]{3,2,1,0:T(8,128)}, u32[]{:S(2)}) copy-start(f32[2,8,64,512]{3,2,1,0:T(8,128)} %multiply_add_fusion) | copy-start | bytes 6291460
  693.7 2.6 copy-start.1
where the time goes:
time: 707 us; the launch traced here: 696 us
  local copies, waits for them, and re-layouts  266 us (38%)
  waiting for transfers between devices  160 us (23%)
  matrix products  136 us (19%)
  starting transfers between devices  67.9 us (10%)
  other arithmetic  65.1 us (9%)
    unnamed x75, local copies, waits for them, and re-layouts  99.1 us
    all_to_all x1, waiting for transfers between devices, on_device(): lax.all_to_all(slope_real, 'col', split_axis=0, concat_axis=3, tiled=True)  33.2 us
    all_to_all x1, waiting for transfers between devices, on_device(): lax.all_to_all(value_real, 'col', split_axis=0, concat_axis=3, tiled=True)  33.1 us
    all_to_all x1, waiting for transfers between devices, on_device(): lax.all_to_all(value_imag, 'col', split_axis=0, concat_axis=3, tiled=True)  33 us
    all_to_all x1, waiting for transfers between devices, on_device(): lax.all_to_all(lax.all_to_all(spectra_imag, 'row', split_axis=3, concat_a...  25.6 us
    dot_general x8, matrix products, contract(): jnp.einsum(form, left_imag, right_imag, precision=highest)  24.6 us
    all_to_all x1, waiting for transfers between devices, on_device(): lax.all_to_all(slope_imag, 'col', split_axis=0, concat_axis=3, tiled=True)  22.4 us
    dot_general x8, matrix products, contract(): jnp.einsum(form, left_real, right_real, precision=highest)  21.7 us
  transfers between devices with their start and end apart: 12, of which 7 were waited for; matrix products, arithmetic and copies ran while one was open for 47% of the time, Pallas kernels for 0%

commit v1 on v0

--- a/solution.py
+++ b/solution.py
@@ -75,6 +75,24 @@
     implicit_rates,
     time_step,
 ):
+
+    def heaps_report(body):
+        current_value, block_out = (lax.psum(1, "col"), lax.axis_index("col"))
+        after = body.shape[0] // current_value
+        placed = list(body.shape)
+        placed[0] = after
+        found_now = placed[3]
+        placed[3] = found_now * current_value
+        local_next = jnp.zeros(placed, body.dtype)
+        for s in range(current_value):
+            low = lax.dynamic_slice_in_dim(body, (block_out ^ s) * after, after, axis=0)
+            if s:
+                low = lax.ppermute(low, "col", [(at, at ^ s) for at in range(current_value)])
+            local_next = lax.dynamic_update_slice_in_dim(
+                local_next, low, (block_out ^ s) * found_now, axis=3
+            )
+        return local_next
+
     row_count = lax.axis_size("row")
     col_count = lax.axis_size("col")
     local_waves = coefficients.shape[3]
@@ -90,7 +108,7 @@
     slope_imag = jnp.einsum("sqpj,zj->zsqp", coefficients[:, 1], mode_slopes, precision=highest)
     fields = (
         lax.all_to_all(value_real, "col", split_axis=0, concat_axis=3, tiled=True),
-        lax.all_to_all(value_imag, "col", split_axis=0, concat_axis=3, tiled=True),
+        heaps_report(value_imag),
         lax.all_to_all(slope_real, "col", split_axis=0, concat_axis=3, tiled=True),
         lax.all_to_all(slope_imag, "col", split_axis=0, concat_axis=3, tiled=True),
     )

time: 707 us -> 843 us (1.19)
  waiting for transfers between devices: 160 us -> 251 us
  local copies, waits for them, and re-layouts: 266 us -> 304 us
  starting transfers between devices: 67.9 us -> 84.2 us
    ppermute x0 -> x15, waiting for transfers between devices: none -> 130 us  [heaps_report(): lax.ppermute(low, 'col', [(at, at ^ s) for at in range(current_value)])]
    dynamic_update_slice x0 -> x16, local copies, waits for them, and re-layouts: none -> 47.9 us  [heaps_report(): lax.dynamic_update_slice_in_dim(local_next, low, (block_out ^ s) * found_...]
    all_to_all x1 -> x0, waiting for transfers between devices: 33 us -> none  [on_device(): lax.all_to_all(value_imag, 'col', split_axis=0, concat_axis=3, tiled=True)]
    ppermute x0 -> x15, starting transfers between devices: none -> 17.6 us  [heaps_report(): lax.ppermute(low, 'col', [(at, at ^ s) for at in range(current_value)])]
    all_to_all x2 -> x0, local copies, waits for them, and re-layouts: 11.8 us -> none  [on_device(): lax.all_to_all(value_imag, 'col', split_axis=0, concat_axis=3, tiled=True)]
    ppermute x0 -> x15, local copies, waits for them, and re-layouts: none -> 10.1 us  [heaps_report(): lax.ppermute(low, 'col', [(at, at ^ s) for at in range(current_value)])]
    unnamed x75 -> x97, local copies, waits for them, and re-layouts: 99.1 us -> 92.6 us
  transfers between devices with their start and end apart: 12 -> 26, of which waited for: 7 -> 14; matrix products, arithmetic and copies ran while one was open for 47% -> 43% of each run, Pallas kernels for 0% -> 0%
where the time goes in v1:
time: 843 us; the launch traced here: 833 us
  local copies, waits for them, and re-layouts  304 us (36%)
  waiting for transfers between devices  251 us (30%)
  matrix products  135 us (16%)
  starting transfers between devices  84.2 us (10%)
  other arithmetic  57.3 us (7%)
    ppermute x15, waiting for transfers between devices, heaps_report(): lax.ppermute(low, 'col', [(at, at ^ s) for at in range(current_value)])  130 us
    unnamed x97, local copies, waits for them, and re-layouts  92.6 us
    dynamic_update_slice x16, local copies, waits for them, and re-layouts, heaps_report(): lax.dynamic_update_slice_in_dim(local_next, low, (block_out ^ s) * found_...  47.9 us
    all_to_all x1, waiting for transfers between devices, on_device(): lax.all_to_all(slope_real, 'col', split_axis=0, concat_axis=3, tiled=True)  33.1 us
    all_to_all x1, waiting for transfers between devices, on_device(): lax.all_to_all(value_real, 'col', split_axis=0, concat_axis=3, tiled=True)  33.1 us
    all_to_all x1, waiting for transfers between devices, on_device(): lax.all_to_all(lax.all_to_all(spectra_imag, 'row', split_axis=3, concat_a...  25.4 us
    dot_general x8, matrix products, contract(): jnp.einsum(form, left_imag, right_imag, precision=highest)  23 us
    dot_general x8, matrix products, contract(): jnp.einsum(form, left_real, right_real, precision=highest)  21.9 us
  transfers between devices with their start and end apart: 26, of which 14 were waited for; matrix products, arithmetic and copies ran while one was open for 43% of the time, Pallas kernels for 0%

profile of v1, /device:TPU:15, one launch (start us, length us, event | category | flops | bytes accessed | tf_op | source)
XLA Modules:
  0.0 833.4 jit_solution(10487942545330814953)
XLA Ops:
  15.2 9.1 %collective-permute-done.1 = f32[32,2,8,64]{0,3,2,1:T(8,128)S(1)} collective-permute-done((f32[32,2,8,64]{0,3,2,1:T(8,128)S(1)}, f32[32,2,8,64]{0,3,2,1:T(8,128)S(1)}, u32[]{:S(2)}, u32[]{:S(2)}) %collective-permute-start.1) | collective-permute-done | bytes 131104 | tf_op jit(solution)/shard_map/ppermute | solution.py:90
  26.3 9.6 %collective-permute-done.2 = f32[32,2,8,64]{0,3,2,1:T(8,128)S(1)} collective-permute-done((f32[32,2,8,64]{0,3,2,1:T(8,128)S(1)}, f32[32,2,8,64]{0,3,2,1:T(8,128)S(1)}, u32[]{:S(2)}, u32[]{:S(2)}) %collective-permute-start.2) | collective-permute-done | bytes 131104 | tf_op jit(solution)/shard_map/ppermute | solution.py:90
  40.8 27.9 %collective-permute-done.5 = f32[32,2,8,64]{0,3,2,1:T(8,128)S(1)} collective-permute-done((f32[32,2,8,64]{0,3,2,1:T(8,128)S(1)}, f32[32,2,8,64]{0,3,2,1:T(8,128)S(1)}, u32[]{:S(2)}, u32[]{:S(2)}) %collective-permute-start.5) | collective-permute-done | bytes 131104 | tf_op jit(solution)/shard_map/ppermute | solution.py:90
  73.3 6.7 collective-permute-done.6
  82.6 45.7 %collective-permute-done.8 = f32[32,2,8,64]{0,3,2,1:T(8,128)S(1)} collective-permute-done((f32[32,2,8,64]{0,3,2,1:T(8,128)S(1)}, f32[32,2,8,64]{0,3,2,1:T(8,128)S(1)}, u32[]{:S(2)}, u32[]{:S(2)}) %collective-permute-start.8) | collective-permute-done | bytes 131104 | tf_op jit(solution)/shard_map/ppermute | solution.py:90
  128.3 22.5 %collective-permute-done.9 = f32[32,2,8,64]{0,3,2,1:T(8,128)S(1)} collective-permute-done((f32[32,2,8,64]{0,3,2,1:T(8,128)S(1)}, f32[32,2,8,64]{0,3,2,1:T(8,128)S(1)}, u32[]{:S(2)}, u32[]{:S(2)}) %collective-permute-start.9) | collective-permute-done | bytes 131104 | tf_op jit(solution)/shard_map/ppermute | solution.py:90
  212.5 5.8 collective-permute-done.14
  234.5 5.6 reshape.197
  240.1 6.0 all-to-all-done
  246.1 9.5 %all-to-all-start.1 = ((f32[16,1,32768]{2,1,0:T(1,128)}), f32[16,1,32768]{2,1,0:T(1,128)}, u32[]{:S(2)}, u32[]{:S(2)}) async-start(f32[16,1,32768]{2,1,0:T(1,128)} %reshape.197), calls=%async_computation.1 | async-start | bytes 4194304 | tf_op jit(solution)/shard_map/all_to_all | solution.py:110
  264.5 5.5 reshape.193
  270.0 33.1 %all-to-all-done.1 = f32[16,1,32768]{2,1,0:T(1,128)} async-done(((f32[16,1,32768]{2,1,0:T(1,128)}), f32[16,1,32768]{2,1,0:T(1,128)}, u32[]{:S(2)}, u32[]{:S(2)}) %all-to-all-start.1) | async-done | bytes 2097184 | tf_op jit(solution)/shard_map/all_to_all | solution.py:110
  316.9 5.5 reshape.195
  322.4 33.1 %all-to-all-done.3 = f32[16,1,32768]{2,1,0:T(1,128)} async-done(((f32[16,1,32768]{2,1,0:T(1,128)}), f32[16,1,32768]{2,1,0:T(1,128)}, u32[]{:S(2)}, u32[]{:S(2)}) %all-to-all-start.3) | async-done | bytes 2097184 | tf_op jit(solution)/shard_map/all_to_all | solution.py:112
  368.9 7.3 reduce.2
  379.2 6.6 copy.180
  391.1 17.3 %all-to-all-done.5 = f32[16,1,32768]{2,1,0:T(1,128)} async-done(((f32[16,1,32768]{2,1,0:T(1,128)}), f32[16,1,32768]{2,1,0:T(1,128)}, u32[]{:S(2)}, u32[]{:S(2)}) %all-to-all-start.5) | async-done | bytes 2097184 | tf_op jit(solution)/shard_map/all_to_all | solution.py:113
  408.4 6.4 all-to-all-start.2
  422.0 7.3 reduce
  432.3 6.6 copy.181
  438.9 5.6 reshape.191
  444.5 7.3 reduce.1
  454.8 6.6 copy.182
  495.7 5.9 all-to-all-start.6
  583.4 6.4 copy.183
  589.8 8.8 %reshape.203 = f32[2,1,262144]{2,1,0:T(1,128)} reshape(f32[2048,2,4,32]{3,2,1,0:T(4,128)} %bitcast.244) | data formatting | bytes 4194304
  610.8 6.4 copy.187
  617.2 8.8 %reshape.199 = f32[2,1,262144]{2,1,0:T(1,128)} reshape(f32[2048,2,4,32]{3,2,1,0:T(4,128)} %bitcast.245) | data formatting | bytes 4194304
  626.0 6.3 all-to-all-start.9
  632.3 8.1 reduce.5
  640.4 8.3 reshape.204
  648.7 6.9 copy.184
  657.6 7.5 copy.155
  665.1 8.6 %reshape.205 = f32[16,1,32768]{2,1,0:T(1,128)} reshape(f32[1024,2,8,32]{3,2,1,0:T(8,128)} %bitcast.247) | data formatting | bytes 4194304
  673.6 7.7 all-to-all-start.8
  681.4 8.1 reduce.3
  689.5 8.3 reshape.200
  697.7 6.9 copy.188
  706.5 7.5 copy.162
  714.0 8.6 %reshape.201 = f32[16,1,32768]{2,1,0:T(1,128)} reshape(f32[1024,2,8,32]{3,2,1,0:T(8,128)} %bitcast.249) | data formatting | bytes 4194304
  722.6 6.2 all-to-all-done.8
  736.6 7.3 reduce.6
  748.7 7.3 copy.194
  756.0 25.4 %all-to-all-done.10 = f32[16,1,32768]{2,1,0:T(1,128)} async-done(((f32[16,1,32768]{2,1,0:T(1,128)}), f32[16,1,32768]{2,1,0:T(1,128)}, u32[]{:S(2)}, u32[]{:S(2)}) %all-to-all-start.10) | async-done | bytes 2097184 | tf_op jit(solution)/shard_map/all_to_all | solution.py:166
  781.4 7.3 reduce.4
  793.4 6.9 copy.195
  800.3 15.3 %convolution_bitcast_fusion.1 = f32[2,1,8,64,512]{4,3,2,0,1:T(8,128)S(1)} fusion(f32[512,2,8,64]{3,0,2,1:T(8,128)} %bitcast.252, f32[512,512]{1,0:T(8,128)S(1)} %copy-done.19), kind=kOutput, calls=%fused_computation.57 | convolution fusion | flops 3221225472 | bytes 5242880 | tf_op jit(solution)/shard_map/zsqp,jz->sqpj/dot_general | solution.py:174
  815.7 13.3 %convolution_bitcast_fusion = f32[2,1,8,64,512]{4,3,2,0,1:T(8,128)S(1)} fusion(f32[512,2,8,64]{3,0,2,1:T(8,128)S(1)} %bitcast.253, f32[512,512]{1,0:T(8,128)S(1)} %copy-done.19), kind=kOutput, calls=%fused_computation.56 | convolution fusion | flops 3221225472 | bytes 5242880 | tf_op jit(solution)/shard_map/zsqp,jz->sqpj/dot_general | solution.py:175
  (231 shorter events, 317.2 us)
Async XLA Ops:
  10.1 4.2 collective-permute-start
  10.8 13.6 %collective-permute-start.1 = (f32[32,2,8,64]{0,3,2,1:T(8,128)S(1)}, f32[32,2,8,64]{0,3,2,1:T(8,128)S(1)}, u32[]{:S(2)}, u32[]{:S(2)}) collective-permute-start(f32[32,2,8,64]{0,3,2,1:T(8,128)S(1)} %get-tuple-element.21), channel_id=1, source_target_pairs={{0,2},{1,3},{2,0},{3,1},{4,6},{5,7},{6,4},{7,5},{8,10},{9,11},{10,... | collective-permute-start | bytes 393224 | tf_op jit(solution)/shard_map/ppermute | solution.py:90
  11.0 24.9 %collective-permute-start.2 = (f32[32,2,8,64]{0,3,2,1:T(8,128)S(1)}, f32[32,2,8,64]{0,3,2,1:T(8,128)S(1)}, u32[]{:S(2)}, u32[]{:S(2)}) collective-permute-start(f32[32,2,8,64]{0,3,2,1:T(8,128)S(1)} %get-tuple-element.20), channel_id=1, source_target_pairs={{0,3},{1,2},{2,1},{3,0},{4,7},{5,6},{6,5},{7,4},{8,11},{9,10},{10,... | collective-permute-start | bytes 393224 | tf_op jit(solution)/shard_map/ppermute | solution.py:90
  12.4 25.9 %collective-permute-start.3 = (f32[32,2,8,64]{0,3,2,1:T(8,128)S(1)}, f32[32,2,8,64]{0,3,2,1:T(8,128)S(1)}, u32[]{:S(2)}, u32[]{:S(2)}) collective-permute-start(f32[32,2,8,64]{0,3,2,1:T(8,128)S(1)} %get-tuple-element.19), channel_id=1, source_target_pairs={{0,4},{1,5},{2,6},{3,7},{4,0},{5,1},{6,2},{7,3},{8,12},{9,13},{10,... | collective-permute-start | bytes 393224 | tf_op jit(solution)/shard_map/ppermute | solution.py:90
  12.6 25.9 %collective-permute-start.4 = (f32[32,2,8,64]{0,3,2,1:T(8,128)S(1)}, f32[32,2,8,64]{0,3,2,1:T(8,128)S(1)}, u32[]{:S(2)}, u32[]{:S(2)}) collective-permute-start(f32[32,2,8,64]{0,3,2,1:T(8,128)S(1)} %get-tuple-element.18), channel_id=1, source_target_pairs={{0,5},{1,4},{2,7},{3,6},{4,1},{5,0},{6,3},{7,2},{8,13},{9,12},{10,... | collective-permute-start | bytes 393224 | tf_op jit(solution)/shard_map/ppermute | solution.py:90
  15.1 53.6 %collective-permute-start.5 = (f32[32,2,8,64]{0,3,2,1:T(8,128)S(1)}, f32[32,2,8,64]{0,3,2,1:T(8,128)S(1)}, u32[]{:S(2)}, u32[]{:S(2)}) collective-permute-start(f32[32,2,8,64]{0,3,2,1:T(8,128)S(1)} %get-tuple-element.17), channel_id=1, source_target_pairs={{0,6},{1,7},{2,4},{3,5},{4,2},{5,3},{6,0},{7,1},{8,14},{9,15},{10,... | collective-permute-start | bytes 393224 | tf_op jit(solution)/shard_map/ppermute | solution.py:90
  25.1 54.8 %collective-permute-start.6 = (f32[32,2,8,64]{0,3,2,1:T(8,128)S(1)}, f32[32,2,8,64]{0,3,2,1:T(8,128)S(1)}, u32[]{:S(2)}, u32[]{:S(2)}) collective-permute-start(f32[32,2,8,64]{0,3,2,1:T(8,128)S(1)} %get-tuple-element.16), channel_id=1, source_target_pairs={{0,7},{1,6},{2,5},{3,4},{4,3},{5,2},{6,1},{7,0},{8,15},{9,14},{10,... | collective-permute-start | bytes 393224 | tf_op jit(solution)/shard_map/ppermute | solution.py:90
  35.9 114.8 %copy-start.26 = (f32[32,2,8,64]{0,3,2,1:T(8,128)}, f32[32,2,8,64]{0,3,2,1:T(8,128)S(1)}, u32[]{:S(2)}) copy-start(f32[32,2,8,64]{0,3,2,1:T(8,128)S(1)} %collective-permute-done.2) | copy-start | bytes 393220
  35.9 44.2 %collective-permute-start.7 = (f32[32,2,8,64]{0,3,2,1:T(8,128)S(1)}, f32[32,2,8,64]{0,3,2,1:T(8,128)S(1)}, u32[]{:S(2)}, u32[]{:S(2)}) collective-permute-start(f32[32,2,8,64]{0,3,2,1:T(8,128)S(1)} %get-tuple-element.15), channel_id=1, source_target_pairs={{0,8},{1,9},{2,10},{3,11},{4,12},{5,13},{6,14},{7,15},{8,0},{9,1},... | collective-permute-start | bytes 393224 | tf_op jit(solution)/shard_map/ppermute | solution.py:90
  38.3 90.0 %collective-permute-start.8 = (f32[32,2,8,64]{0,3,2,1:T(8,128)S(1)}, f32[32,2,8,64]{0,3,2,1:T(8,128)S(1)}, u32[]{:S(2)}, u32[]{:S(2)}) collective-permute-start(f32[32,2,8,64]{0,3,2,1:T(8,128)S(1)} %get-tuple-element.14), channel_id=1, source_target_pairs={{0,9},{1,8},{2,11},{3,10},{4,13},{5,12},{6,15},{7,14},{8,1},{9,0},... | collective-permute-start | bytes 393224 | tf_op jit(solution)/shard_map/ppermute | solution.py:90
  38.5 112.3 %collective-permute-start.9 = (f32[32,2,8,64]{0,3,2,1:T(8,128)S(1)}, f32[32,2,8,64]{0,3,2,1:T(8,128)S(1)}, u32[]{:S(2)}, u32[]{:S(2)}) collective-permute-start(f32[32,2,8,64]{0,3,2,1:T(8,128)S(1)} %get-tuple-element.13), channel_id=1, source_target_pairs={{0,10},{1,11},{2,8},{3,9},{4,14},{5,15},{6,12},{7,13},{8,2},{9,3},... | collective-permute-start | bytes 393224 | tf_op jit(solution)/shard_map/ppermute | solution.py:90
  68.7 82.1 %copy-start.24 = (f32[32,2,8,64]{0,3,2,1:T(8,128)}, f32[32,2,8,64]{0,3,2,1:T(8,128)S(1)}, u32[]{:S(2)}) copy-start(f32[32,2,8,64]{0,3,2,1:T(8,128)S(1)} %collective-permute-done.5) | copy-start | bytes 393220
  68.7 123.9 %collective-permute-start.10 = (f32[32,2,8,64]{0,3,2,1:T(8,128)}, f32[32,2,8,64]{0,3,2,1:T(8,128)}, u32[]{:S(2)}, u32[]{:S(2)}) collective-permute-start(f32[32,2,8,64]{0,3,2,1:T(8,128)} %get-tuple-element.12), channel_id=1, source_target_pairs={{0,11},{1,10},{2,9},{3,8},{4,15},{5,14},{6,13},{7,12},{8,3},{9,2},... | collective-permute-start | bytes 393224 | tf_op jit(solution)/shard_map/ppermute | solution.py:90
  80.0 70.8 %copy-start.27 = (f32[32,2,8,64]{0,3,2,1:T(8,128)}, f32[32,2,8,64]{0,3,2,1:T(8,128)S(1)}, u32[]{:S(2)}) copy-start(f32[32,2,8,64]{0,3,2,1:T(8,128)S(1)} %collective-permute-done.6) | copy-start | bytes 393220
  80.0 115.8 %collective-permute-start.11 = (f32[32,2,8,64]{0,3,2,1:T(8,128)}, f32[32,2,8,64]{0,3,2,1:T(8,128)}, u32[]{:S(2)}, u32[]{:S(2)}) collective-permute-start(f32[32,2,8,64]{0,3,2,1:T(8,128)} %get-tuple-element.11), channel_id=1, source_target_pairs={{0,12},{1,13},{2,14},{3,15},{4,8},{5,9},{6,10},{7,11},{8,4},{9,5},... | collective-permute-start | bytes 393224 | tf_op jit(solution)/shard_map/ppermute | solution.py:90
  80.1 70.7 %copy-start.30 = (f32[32,2,8,64]{0,3,2,1:T(8,128)}, f32[32,2,8,64]{0,3,2,1:T(8,128)S(1)}, u32[]{:S(2)}) copy-start(f32[32,2,8,64]{0,3,2,1:T(8,128)S(1)} %collective-permute-done.7) | copy-start | bytes 393220
  80.1 121.0 %collective-permute-start.12 = (f32[32,2,8,64]{0,3,2,1:T(8,128)}, f32[32,2,8,64]{0,3,2,1:T(8,128)}, u32[]{:S(2)}, u32[]{:S(2)}) collective-permute-start(f32[32,2,8,64]{0,3,2,1:T(8,128)} %get-tuple-element.10), channel_id=1, source_target_pairs={{0,13},{1,12},{2,15},{3,14},{4,9},{5,8},{6,11},{7,10},{8,5},{9,4},... | collective-permute-start | bytes 393224 | tf_op jit(solution)/shard_map/ppermute | solution.py:90
  128.3 22.5 %copy-start.33 = (f32[32,2,8,64]{0,3,2,1:T(8,128)}, f32[32,2,8,64]{0,3,2,1:T(8,128)S(1)}, u32[]{:S(2)}) copy-start(f32[32,2,8,64]{0,3,2,1:T(8,128)S(1)} %collective-permute-done.8) | copy-start | bytes 393220
  128.3 78.8 %collective-permute-start.13 = (f32[32,2,8,64]{0,3,2,1:T(8,128)}, f32[32,2,8,64]{0,3,2,1:T(8,128)}, u32[]{:S(2)}, u32[]{:S(2)}) collective-permute-start(f32[32,2,8,64]{0,3,2,1:T(8,128)} %get-tuple-element.9), channel_id=1, source_target_pairs={{0,14},{1,15},{2,12},{3,13},{4,10},{5,11},{6,8},{7,9},{8,6},{9,7},... | collective-permute-start | bytes 393224 | tf_op jit(solution)/shard_map/ppermute | solution.py:90
  151.6 66.7 %collective-permute-start.14 = (f32[32,2,8,64]{0,3,2,1:T(8,128)}, f32[32,2,8,64]{0,3,2,1:T(8,128)S(1)}, u32[]{:S(2)}, u32[]{:S(2)}) collective-permute-start(f32[32,2,8,64]{0,3,2,1:T(8,128)} %get-tuple-element.8), channel_id=1, source_target_pairs={{0,15},{1,14},{2,13},{3,12},{4,11},{5,10},{6,9},{7,8},{8,7},{9,6},... | collective-permute-start | bytes 393224 | tf_op jit(solution)/shard_map/ppermute | solution.py:90
  166.4 9.7 %copy-start.25 = (f32[32,2,8,64]{0,3,2,1:T(8,128)S(1)}, f32[32,2,8,64]{0,3,2,1:T(8,128)}, u32[]{:S(2)}) copy-start(f32[32,2,8,64]{0,3,2,1:T(8,128)} %copy-done.24) | copy-start | bytes 393220
  169.7 10.8 %copy-start.28 = (f32[32,2,8,64]{0,3,2,1:T(8,128)S(1)}, f32[32,2,8,64]{0,3,2,1:T(8,128)}, u32[]{:S(2)}) copy-start(f32[32,2,8,64]{0,3,2,1:T(8,128)} %copy-done.27) | copy-start | bytes 393220
  174.1 8.4 %copy-start.31 = (f32[32,2,8,64]{0,3,2,1:T(8,128)S(1)}, f32[32,2,8,64]{0,3,2,1:T(8,128)}, u32[]{:S(2)}) copy-start(f32[32,2,8,64]{0,3,2,1:T(8,128)} %copy-done.30) | copy-start | bytes 393220
  176.2 10.0 %copy-start.34 = (f32[32,2,8,64]{0,3,2,1:T(8,128)S(1)}, f32[32,2,8,64]{0,3,2,1:T(8,128)}, u32[]{:S(2)}) copy-start(f32[32,2,8,64]{0,3,2,1:T(8,128)} %copy-done.33) | copy-start | bytes 393220
  180.7 7.5 copy-start.36
  220.3 25.7 %all-to-all-start = ((f32[32,2,8,1024]{3,0,1,2:T(8,128)}), f32[32,2,8,1024]{3,0,1,2:T(8,128)}, u32[]{:S(2)}, u32[]{:S(2)}) async-start(f32[32,2,8,1024]{3,0,1,2:T(8,128)} %dynamic_update_slice.63), calls=%async_computation | async-start | bytes 4194304 | tf_op jit(solution)/shard_map/all_to_all | solution.py:117
  240.1 15.5 %copy-start.18 = (f32[512,512]{1,0:T(8,128)S(1)}, f32[512,512]{1,0:T(8,128)}, u32[]{:S(2)}) copy-start(f32[512,512]{1,0:T(8,128)} %param.12) | copy-start | bytes 3145732
  246.1 57.0 %all-to-all-start.1 = ((f32[16,1,32768]{2,1,0:T(1,128)}), f32[16,1,32768]{2,1,0:T(1,128)}, u32[]{:S(2)}, u32[]{:S(2)}) async-start(f32[16,1,32768]{2,1,0:T(1,128)} %reshape.197), calls=%async_computation.1 | async-start | bytes 4194304 | tf_op jit(solution)/shard_map/all_to_all | solution.py:110
  303.1 52.4 %all-to-all-start.3 = ((f32[16,1,32768]{2,1,0:T(1,128)}), f32[16,1,32768]{2,1,0:T(1,128)}, u32[]{:S(2)}, u32[]{:S(2)}) async-start(f32[16,1,32768]{2,1,0:T(1,128)} %reshape.193), calls=%async_computation.3 | async-start | bytes 4194304 | tf_op jit(solution)/shard_map/all_to_all | solution.py:112
  322.4 38.6 %copy-start.23 = (f32[3,32,2048]{2,1,0:T(8,128)S(1)}, f32[3,32,2048]{2,1,0:T(8,128)}, u32[]{:S(2)}) copy-start(f32[3,32,2048]{2,1,0:T(8,128)} %param.15) | copy-start | bytes 2359300
  355.6 52.8 %all-to-all-start.5 = ((f32[16,1,32768]{2,1,0:T(1,128)}), f32[16,1,32768]{2,1,0:T(1,128)}, u32[]{:S(2)}, u32[]{:S(2)}) async-start(f32[16,1,32768]{2,1,0:T(1,128)} %reshape.195), calls=%async_computation.5 | async-start | bytes 4194304 | tf_op jit(solution)/shard_map/all_to_all | solution.py:113
  391.1 24.9 %copy-start.22 = (f32[32,16,128]{2,1,0:T(8,128)S(1)}, f32[32,16,128]{2,1,0:T(8,128)}, u32[]{:S(2)}) copy-start(f32[32,16,128]{2,1,0:T(8,128)} %copy.138) | copy-start | bytes 786436
  408.4 58.3 %all-to-all-start.2 = ((f32[32,2,8,1024]{3,1,0,2:T(2,128)}), f32[32,2,8,1024]{3,1,0,2:T(2,128)}, u32[]{:S(2)}, u32[]{:S(2)}) async-start(f32[32,2,8,1024]{3,1,0,2:T(2,128)} %reshape.190), calls=%async_computation.2 | async-start | bytes 4194304 | tf_op jit(solution)/shard_map/all_to_all | solution.py:116
  466.6 29.0 %all-to-all-start.4 = ((f32[32,2,8,1024]{3,1,0,2:T(2,128)}), f32[32,2,8,1024]{3,1,0,2:T(2,128)}, u32[]{:S(2)}, u32[]{:S(2)}) async-start(f32[32,2,8,1024]{3,1,0,2:T(2,128)} %reshape.191), calls=%async_computation.4 | async-start | bytes 4194304 | tf_op jit(solution)/shard_map/all_to_all | solution.py:118
  495.7 30.2 %all-to-all-start.6 = ((f32[32,2,8,1024]{3,1,0,2:T(2,128)}), f32[32,2,8,1024]{3,1,0,2:T(2,128)}, u32[]{:S(2)}, u32[]{:S(2)}) async-start(f32[32,2,8,1024]{3,1,0,2:T(2,128)} %reshape.192), calls=%async_computation.6 | async-start | bytes 4194304 | tf_op jit(solution)/shard_map/all_to_all | solution.py:119
  510.8 4.9 copy-start.10
  535.2 4.4 copy-start.9
  535.2 4.4 copy-start.12
  598.6 27.4 %all-to-all-start.7 = ((f32[2,1,262144]{2,1,0:T(1,128)}), f32[2,1,262144]{2,1,0:T(1,128)}, u32[]{:S(2)}, u32[]{:S(2)}) async-start(f32[2,1,262144]{2,1,0:T(1,128)} %reshape.203), calls=%async_computation.7 | async-start | bytes 4194304 | tf_op jit(solution)/shard_map/all_to_all | solution.py:160
  626.0 47.6 %all-to-all-start.9 = ((f32[2,1,262144]{2,1,0:T(1,128)}), f32[2,1,262144]{2,1,0:T(1,128)}, u32[]{:S(2)}, u32[]{:S(2)}) async-start(f32[2,1,262144]{2,1,0:T(1,128)} %reshape.199), calls=%async_computation.9 | async-start | bytes 4194304 | tf_op jit(solution)/shard_map/all_to_all | solution.py:167
  673.6 55.1 %all-to-all-start.8 = ((f32[16,1,32768]{2,1,0:T(1,128)}), f32[16,1,32768]{2,1,0:T(1,128)}, u32[]{:S(2)}, u32[]{:S(2)}) async-start(f32[16,1,32768]{2,1,0:T(1,128)} %reshape.205), calls=%async_computation.8 | async-start | bytes 4194304 | tf_op jit(solution)/shard_map/all_to_all | solution.py:159
  722.6 12.1 %copy-start.37 = (f32[512]{0:T(512)S(1)}, f32[512]{0:T(512)}, u32[]{:S(2)}) copy-start(f32[512]{0:T(512)} %param.14) | copy-start | bytes 6148
  722.6 12.4 %copy-start.39 = (f32[2]{0:T(128)S(1)}, f32[2]{0:T(128)}, u32[]{:S(2)}) copy-start(f32[2]{0:T(128)} %param.18) | copy-start | bytes 28
  728.7 52.6 %all-to-all-start.10 = ((f32[16,1,32768]{2,1,0:T(1,128)}), f32[16,1,32768]{2,1,0:T(1,128)}, u32[]{:S(2)}, u32[]{:S(2)}) async-start(f32[16,1,32768]{2,1,0:T(1,128)} %reshape.201), calls=%async_computation.10 | async-start | bytes 4194304 | tf_op jit(solution)/shard_map/all_to_all | solution.py:166
  793.4 6.9 copy-start.19
  800.3 15.3 %copy-start.11 = (f32[16,32,2,8,64]{4,1,0,3,2:T(8,128)S(1)}, f32[16,32,2,8,64]{4,1,0,3,2:T(8,128)}, u32[]{:S(2)}) copy-start(f32[16,32,2,8,64]{4,1,0,3,2:T(8,128)} %copy.195) | copy-start | bytes 6291460
  815.6 13.4 %copy-start.2 = (f32[2,2,8,64,512]{4,3,2,1,0:T(8,128)S(1)}, f32[2,2,8,64,512]{4,3,2,1,0:T(8,128)}, u32[]{:S(2)}) copy-start(f32[2,2,8,64,512]{4,3,2,1,0:T(8,128)} %param.10) | copy-start | bytes 12582916
  815.7 13.4 %copy-start.15 = (f32[2,8,64,512]{3,2,1,0:T(8,128)S(1)}, f32[2,8,64,512]{3,2,1,0:T(8,128)}, u32[]{:S(2)}) copy-start(f32[2,8,64,512]{3,2,1,0:T(8,128)} %multiply_add_fusion) | copy-start | bytes 6291460
  (19 other events, 41.1 us)
